TPU v7x, 512 devices: a whole 4x4x16 slice. The times are simulated.
512 devices in a mesh: pipe: 16 (over z), tp: 32 (over x, y, core).
Axes of the slice: x: 4, y: 4, z: 16, core: 2. Of those that a mesh axis runs over, the one named last changes fastest.
Arguments:
- stream: bfloat16 [16, 2048, 4096], P('pipe', None, 'tp')
- incoming: bfloat16 [1, 2048, 4096], P(None, None, 'tp')
- chosen: int32 [16, 2, 512], P('pipe'), may hold values from 0 to 2047, as said below
- live: int32 [16, 2], P('pipe'), may hold values from 256 to 512, as said below
- norm_gain: float32 [16, 4096], P('pipe'), may hold values from 0.1 to 1.9
- router: bfloat16 [16, 4096], P('pipe'), may hold values from -0.09375 to 0.09375
- wq: bfloat16 [16, 4096, 4096], P('pipe', None, 'tp')
- wk: bfloat16 [16, 4096, 1024], P('pipe', None, 'tp')
- wv: bfloat16 [16, 4096, 1024], P('pipe', None, 'tp'), may hold values from -0.09375 to 0.09375
- wo: bfloat16 [16, 4096, 4096], P('pipe', None, 'tp'), may hold values from -0.09375 to 0.09375
Outputs:
- advanced: bfloat16 [16, 2048, 4096], P('pipe', None, 'tp')
Inputs may be any that keep to these rules, and one draw needn't show every extreme that they name: `chosen`: each list holds 512 distinct token positions in increasing order. `live`: at every tick some section's list is full.
All inputs are finite; a program needn't handle non-finite values.
Results may differ from a plain program's by a relative error of at most 0.0025.
Values may be sent and summed in bfloat16 or wider, within the bound.
A program may use at most 64 MiB of HBM per device.

v0:
```python
import math

import jax
import jax.numpy as jnp
from jax import lax
from jax.sharding import PartitionSpec as P

KVH = 8
HD = 128


def from_partner(value, axis, stride):
    mask = 2**stride
    pairs = [(source, source ^ mask) for source in range(lax.axis_size(axis))]
    return lax.ppermute(value, axis, pairs)


def from_behind(block, axis, distance):
    devices = range(lax.axis_size(axis))
    route = [(i - distance, i) for i in devices if i - distance in devices]
    return lax.ppermute(block, axis, route)


def rotate(values, position):
    half = values.shape[-1] // 2
    freq = jnp.exp(
        -math.log(500000.0) * 2.0 * jnp.arange(half, dtype=jnp.float32) / values.shape[-1]
    )
    angle = position[:, None] * freq[None, :]
    cosine = jnp.cos(angle)[:, None, :]
    sine = jnp.sin(angle)[:, None, :]
    first = values[..., :half]
    second = values[..., half:]
    return jnp.concatenate(
        [first * cosine - second * sine, second * cosine + first * sine], axis=-1
    )


def project_rows(picked, gain, route, w_query, w_key, w_value):
    gathered = lax.all_gather(picked, "tp", axis=1, tiled=True)
    widened = gathered.astype(jnp.float32)
    square_sum = jnp.sum(widened * widened, axis=1)
    scaled = (widened * gain).astype(jnp.bfloat16)
    query_sum = jnp.dot(scaled, w_query, preferred_element_type=jnp.float32)
    key_sum = jnp.dot(scaled, w_key, preferred_element_type=jnp.float32)
    value_sum = jnp.dot(scaled, w_value, preferred_element_type=jnp.float32)
    logit_sum = jnp.dot(scaled, route, preferred_element_type=jnp.float32)
    rstd = lax.rsqrt(square_sum / gain.shape[0] + 1e-05)
    return (query_sum, key_sum, value_sum, logit_sum, rstd)


def head_columns(key_lin, value_lin):
    pair = jnp.stack([key_lin, value_lin])
    rank = lax.axis_index("tp")
    group = lax.axis_size("tp") // KVH
    for bit in range(group.bit_length() - 1):
        other = from_partner(pair, "tp", bit)
        lower = rank >> bit & 1 == 0
        pair = jnp.where(
            lower, jnp.concatenate([pair, other], axis=2), jnp.concatenate([other, pair], axis=2)
        )
    return pair


def routed_block(state, index, count, gain, route, w_query, w_key, w_value, w_out):
    picked = jnp.take(state, index, axis=0)
    cap = picked.shape[0]
    position = index.astype(jnp.float32)
    query_sum, key_sum, value_sum, logit_sum, rstd = project_rows(
        picked, gain, route, w_query, w_key, w_value
    )
    logit = logit_sum * rstd
    query = rotate((query_sum * rstd[:, None]).reshape(cap, -1, HD), position).astype(jnp.bfloat16)
    key_lin = (key_sum * rstd[:, None]).astype(jnp.bfloat16)
    value_lin = (value_sum * rstd[:, None]).astype(jnp.bfloat16)
    both = head_columns(key_lin, value_lin)
    keys = rotate(both[0][:, None, :].astype(jnp.float32), position)[:, 0, :].astype(jnp.bfloat16)
    values = both[1]
    scores = jnp.einsum("qhd,kd->hqk", query, keys, preferred_element_type=jnp.float32) / math.sqrt(
        HD
    )
    slots = jnp.arange(cap)
    allowed = (slots[None, :] <= slots[:, None]) & (slots[None, :] < count)
    scores = jnp.where(allowed[None], scores, -jnp.inf)
    top = jnp.max(scores, axis=-1, keepdims=True)
    weights = jnp.exp(scores - top)
    probs = (weights / jnp.sum(weights, axis=-1, keepdims=True)).astype(jnp.bfloat16)
    attended = jnp.einsum("hqk,kd->qhd", probs, values, preferred_element_type=jnp.float32)
    attended = attended.astype(jnp.bfloat16).reshape(cap, -1)
    delta = jnp.dot(
        lax.all_gather(attended, "tp", axis=1, tiled=True),
        w_out,
        preferred_element_type=jnp.float32,
    )
    mixing = jax.nn.sigmoid(logit) * (slots < count).astype(jnp.float32)
    updated = (picked.astype(jnp.float32) + mixing[:, None] * delta).astype(jnp.bfloat16)
    return state.at[index].set(updated)


def body(stream, incoming, chosen, live, norm_gain, router, wq, wk, wv, wo):
    state = stream[0]
    first_section = lax.axis_index("pipe") == 0
    for tick in range(chosen.shape[1]):
        if tick > 0:
            moved = from_behind(state, "pipe", 1)
            state = jnp.where(first_section, incoming[tick - 1], moved)
        state = routed_block(
            state,
            chosen[0, tick],
            live[0, tick],
            norm_gain[0],
            router[0],
            wq[0],
            wk[0],
            wv[0],
            wo[0],
        )
    return state[None]


def solution(mesh):
    in_specs = (
        P("pipe", None, "tp"),
        P(None, None, "tp"),
        P("pipe", None, None),
        P("pipe", None),
        P("pipe", None),
        P("pipe", None),
        P("pipe", None, "tp"),
        P("pipe", None, "tp"),
        P("pipe", None, "tp"),
        P("pipe", None, "tp"),
    )
    out_specs = P("pipe", None, "tp")
    return jax.shard_map(body, mesh=mesh, in_specs=in_specs, out_specs=out_specs, check_vma=False)
```

profile of v0, /device:TPU:1, one launch (start us, length us, event | category | flops | bytes accessed | tf_op | source)
XLA Modules:
  0.0 347.6 jit_solution(17755792798985170252)
XLA Ops:
  6.5 1.1 copy.14
  7.7 0.8 fusion.157
  8.5 1.3 gather_fusion
  9.8 0.8 broadcast_select_fusion.1
  10.7 1.4 fusion.158
  12.1 69.0 %all-gather.7.cloned.1.call-done = bf16[512,4096]{1,0:T(8,128)(2,1)} async-done(((bf16[512,128]{1,0:T(8,128)(2,1)}), bf16[512,4096]{1,0:T(8,128)(2,1)}) %all-gather.7.cloned.1.call-update) | async-done | bytes 4194320 | tf_op jit(solution)/shard_map/all_gather | solution.py:40
  81.1 3.2 fusion.1
  84.5 1.2 fusion.22
  85.7 0.7 divide_select_fusion.1
  86.4 1.4 fusion.81
  87.8 1.4 fusion.78
  89.2 2.2 collective-permute-start
  91.3 0.6 iota_compare_fusion.2
  92.0 0.3 collective-permute-done
  92.3 2.8 collective-permute-start.1
  95.1 1.5 fusion.40
  96.7 2.4 collective-permute-done.1
  99.2 0.6 fusion.152
  99.8 0.3 fusion.159
  100.2 0.2 fusion.96
  100.4 1.0 fusion.52
  101.5 61.9 %all-gather.11.cloned.1.call-done = bf16[512,1,4096]{0,2,1:T(8,128)(2,1)} async-done(((bf16[512,1,128]{0,2,1:T(8,128)(2,1)}), bf16[512,1,4096]{0,2,1:T(8,128)(2,1)}) %all-gather.11.cloned.1.call-update) | async-done | bytes 4194320 | tf_op jit(solution)/shard_map/all_gather | solution.py:91
  163.4 3.5 %fusion.49 = bf16[512,128]{1,0:T(8,128)(2,1)S(1)} fusion(bf16[512,1,4096]{0,2,1:T(8,128)(2,1)} %all-gather.11.cloned.1.call-done, bf16[1,4096,128]{2,1,0:T(8,128)(2,1)S(1)} %copy-done.7, bf16[512,128]{1,0:T(8,128)(2,1)S(1)} %copy-done.5, f32[512]{0:T(512)S(1)} %get-tuple-element.24), kind=kOutput, calls=%fused_computation.39 | convolution fusion | flops 537133056 | bytes 5507072 | tf_op jit(solution)/shard_map/dot_general | solution.py:90
  166.9 2.1 scatter_fusion
  168.9 3.2 collective-permute-start.2
  172.2 11.0 %collective-permute-done.2 = bf16[2048,128]{1,0:T(8,128)(2,1)S(1)} collective-permute-done((bf16[2048,128]{1,0:T(8,128)(2,1)S(1)}, bf16[2048,128]{1,0:T(8,128)(2,1)S(1)}, u32[]{:S(2)}, u32[]{:S(2)}) %collective-permute-start.2) | collective-permute-done | bytes 524320 | tf_op jit(solution)/shard_map/ppermute | solution.py:21
  183.3 1.3 gather_fusion.1
  184.6 0.8 broadcast_select_fusion
  185.4 0.2 all-gather.13.cloned.1.call-start
  185.7 66.9 %all-gather.9.cloned.1.call-done = bf16[512,4096]{1,0:T(8,128)(2,1)} async-done(((bf16[512,128]{1,0:T(8,128)(2,1)}), bf16[512,4096]{1,0:T(8,128)(2,1)}) %all-gather.9.cloned.1.call-update) | async-done | bytes 4194320 | tf_op jit(solution)/shard_map/all_gather | solution.py:40
  252.6 3.5 %fusion.14 = f32[1,512]{1,0:T(1,128)S(1)} fusion(bf16[512,4096]{1,0:T(8,128)(2,1)} %all-gather.9.cloned.1.call-done, f32[4096]{0:T(1024)S(1)} %bitcast.144, bf16[1,4096]{1,0:T(2,128)(2,1)S(1)} %copy-done.12), kind=kOutput, calls=%fused_computation.19 | convolution fusion | flops 10485760 | bytes 4220928 | tf_op jit(solution)/shard_map/dot_general | solution.py:47
  256.1 0.9 fusion.3
  257.0 0.7 divide_select_fusion
  257.7 1.4 fusion.87
  259.1 1.4 fusion.84
  260.5 2.2 collective-permute-start.3
  262.6 0.6 iota_compare_fusion.1
  263.3 0.3 collective-permute-done.3
  263.6 2.8 collective-permute-start.4
  266.4 1.5 fusion.46
  268.0 2.4 collective-permute-done.4
  270.5 0.6 fusion.150
  271.1 0.3 fusion.160
  271.6 1.0 fusion.53
  272.6 62.0 %all-gather.13.cloned.1.call-done = bf16[512,1,4096]{0,2,1:T(8,128)(2,1)} async-done(((bf16[512,1,128]{0,2,1:T(8,128)(2,1)}), bf16[512,1,4096]{0,2,1:T(8,128)(2,1)}) %all-gather.13.cloned.1.call-update) | async-done | bytes 4194320 | tf_op jit(solution)/shard_map/all_gather | solution.py:91
  334.6 3.5 fusion.34
  338.1 2.2 scatter_custom_fusion.1
  340.3 0.8 copy-done.1
  (54 shorter events, 1.0 us)
Async XLA Ops:
  6.5 88.6 %copy-start = (bf16[1,4096,128]{2,1,0:T(8,128)(2,1)S(1)}, bf16[1,4096,128]{2,1,0:T(8,128)(2,1)}, u32[]{:S(2)}) copy-start(bf16[1,4096,128]{2,1,0:T(8,128)(2,1)} %param.18) | copy-start | bytes 3145732
  6.5 77.8 %copy-start.13 = (f32[1,4096]{1,0:T(1,128)S(1)}, f32[1,4096]{1,0:T(1,128)}, u32[]{:S(2)}) copy-start(f32[1,4096]{1,0:T(1,128)} %param.16) | copy-start | bytes 49156
  6.5 77.8 %copy-start.12 = (bf16[1,4096]{1,0:T(2,128)(2,1)S(1)}, bf16[1,4096]{1,0:T(2,128)(2,1)}, u32[]{:S(2)}) copy-start(bf16[1,4096]{1,0:T(2,128)(2,1)} %param.17) | copy-start | bytes 24580
  6.5 74.5 %all-gather.7.cloned.1.call-start = ((), (), s32[]{:S(2)}) async-start(), calls=%async_computation | async-start | bytes 4325376 | tf_op jit(solution)/shard_map/all_gather | solution.py:40
  10.6 152.7 %all-gather.11.cloned.1.call-start = ((), (), s32[]{:S(2)}) async-start(), calls=%async_computation.2 | async-start | bytes 4325376 | tf_op jit(solution)/shard_map/all_gather | solution.py:91
  81.1 3.4 copy-start.2
  84.3 2.1 copy-start.8
  85.7 2.1 copy-start.10
  89.2 3.1 collective-permute-start
  92.3 6.7 %collective-permute-start.1 = (bf16[2,512,64]{1,2,0:T(8,128)(2,1)S(1)}, bf16[2,512,64]{1,2,0:T(8,128)(2,1)S(1)}, u32[]{:S(2)}, u32[]{:S(2)}) collective-permute-start(bf16[2,512,64]{1,2,0:T(8,128)(2,1)S(1)} %maximum_select_fusion.2), channel_id=1, source_target_pairs={{0,2},{1,3},{2,0},{3,1},{4,6},{5,7},{6,4},{7,5},{8,10},{9,11},{10,... | collective-permute-start | bytes 393224 | tf_op jit(solution)/shard_map/ppermute | solution.py:15
  99.2 2.3 copy-start.6
  99.2 64.2 %copy-start.5 = (bf16[512,128]{1,0:T(8,128)(2,1)S(1)}, bf16[512,128]{1,0:T(8,128)(2,1)}, u32[]{:S(2)}) copy-start(bf16[512,128]{1,0:T(8,128)(2,1)} %broadcast_select_fusion.1) | copy-start | bytes 393220
  99.2 64.2 %copy-start.7 = (bf16[1,4096,128]{2,1,0:T(8,128)(2,1)S(1)}, bf16[1,4096,128]{2,1,0:T(8,128)(2,1)}, u32[]{:S(2)}) copy-start(bf16[1,4096,128]{2,1,0:T(8,128)(2,1)} %param.21) | copy-start | bytes 3145732
  101.4 81.8 %copy-start.4 = (bf16[1,2048,128]{2,1,0:T(8,128)(2,1)S(1)}, bf16[1,2048,128]{2,1,0:T(8,128)(2,1)}, u32[]{:S(2)}) copy-start(bf16[1,2048,128]{2,1,0:T(8,128)(2,1)} %param.13) | copy-start | bytes 1572868
  101.4 151.2 %all-gather.9.cloned.1.call-start = ((), (), s32[]{:S(2)}) async-start(), calls=%async_computation.1 | async-start | bytes 4325376 | tf_op jit(solution)/shard_map/all_gather | solution.py:40
  168.9 14.2 %collective-permute-start.2 = (bf16[2048,128]{1,0:T(8,128)(2,1)S(1)}, bf16[2048,128]{1,0:T(8,128)(2,1)S(1)}, u32[]{:S(2)}, u32[]{:S(2)}) collective-permute-start(bf16[2048,128]{1,0:T(8,128)(2,1)S(1)} %scatter_fusion), channel_id=1, source_target_pairs={{0,32},{32,64},{64,96},{96,128},{128,160},{160,192},{192,224},{224... | collective-permute-start | bytes 1572872 | tf_op jit(solution)/shard_map/ppermute | solution.py:21
  185.4 149.2 %all-gather.13.cloned.1.call-start = ((), (), s32[]{:S(2)}) async-start(), calls=%async_computation.3 | async-start | bytes 4325376 | tf_op jit(solution)/shard_map/all_gather | solution.py:91
  185.7 72.0 %copy-start.9 = (bf16[1,4096,32]{1,2,0:T(8,128)(2,1)S(1)}, bf16[1,4096,32]{1,2,0:T(8,128)(2,1)}, u32[]{:S(2)}) copy-start(bf16[1,4096,32]{1,2,0:T(8,128)(2,1)} %param.20) | copy-start | bytes 786436
  252.6 3.5 %copy-start.3 = (bf16[512,4096]{1,0:T(8,128)(2,1)S(1)}, bf16[512,4096]{1,0:T(8,128)(2,1)}, u32[]{:S(2)}) copy-start(bf16[512,4096]{1,0:T(8,128)(2,1)} %all-gather.9.cloned.1.call-done) | copy-start | bytes 12582916
  257.0 2.1 copy-start.11
  260.5 3.1 collective-permute-start.3
  263.6 6.7 %collective-permute-start.4 = (bf16[2,512,64]{1,2,0:T(8,128)(2,1)S(1)}, bf16[2,512,64]{1,2,0:T(8,128)(2,1)S(1)}, u32[]{:S(2)}, u32[]{:S(2)}) collective-permute-start(bf16[2,512,64]{1,2,0:T(8,128)(2,1)S(1)} %maximum_select_fusion.3), channel_id=1, source_target_pairs={{0,2},{1,3},{2,0},{3,1},{4,6},{5,7},{6,4},{7,5},{8,10},{9,11},{10,... | collective-permute-start | bytes 393224 | tf_op jit(solution)/shard_map/ppermute | solution.py:15
  340.3 0.8 copy-start.1
Sparse Core Ops, SparseCore 0:
  10.8 70.2 all-gather.6
  101.5 61.8 all-gather.10
  185.5 66.9 all-gather.8
  272.8 61.8 all-gather.12
where the time goes:
time: 348 us
  waiting for transfers between devices  276 us (79%)
  matrix products  22.8 us (7%)
  between operations  13.5 us (4%)
  starting transfers between devices  13.4 us (4%)
  other arithmetic  12.5 us (4%)
  local copies, waits for them, and re-layouts  9.06 us (3%)
    all_gather x2, waiting for transfers between devices, project_rows(): gathered = lax.all_gather(picked, 'tp', axis=1, tiled=True)  136 us
    all_gather x2, waiting for transfers between devices, routed_block(): lax.all_gather(attended, 'tp', axis=1, tiled=True)  124 us
    ppermute x1, waiting for transfers between devices, from_behind(): return lax.ppermute(block, axis, route)  11 us
    ppermute x4, starting transfers between devices, from_partner(): return lax.ppermute(value, axis, pairs)  9.84 us
  transfers between devices with their start and end apart: 9, of which 9 were waited for; matrix products, arithmetic and copies ran while one was open for 2% of the time, Pallas kernels for 0%

commit v1 on v0

v1 whole, which is shorter than its diff:
```python
import functools
import math

import jax
import jax.numpy as jnp
import numpy as np
from jax import lax
from jax.experimental import pallas as pl
from jax.experimental.pallas import tpu as pltpu
from jax.sharding import PartitionSpec as P

MESH = pl.DeviceIdType.MESH
F32 = jnp.float32
BF16 = jnp.bfloat16

D = 4096
TOKENS = 2048
CAP = 512
HD = 128
N = 4
R = CAP // N
H = R // 2


def kernel(
    stream, incoming, chosen, live, gain, router, freq, wq, wk, wv, wo, out,
    strm, inc, bulk, wqa, woa, wkl, wvl, w2o, w2p, w2, lprev, lsp, cosb, sinb, gath, pst, bp, kvb, kc, vc,
    qs, accq, acck, ssb, lgb, mixb, accd, ub, u0, u1s, u1, mt, facc,
    loc, ag_s, ag_r, pk_s, pk_r, kv_s, kv_r, uz_s, uz_r, wx_s, wx_r, e_s, e_r,
):
    z = lax.axis_index("pipe")
    t = lax.axis_index("tp")
    nz = lax.axis_size("pipe")
    c = t % 2
    chip = t // 2
    y = chip % 4
    x = chip // 4
    p = x * (1 - c) + y * c
    q = y * (1 - c) + x * c
    own = q * 4 + p
    partner = (z, chip * 2 + 1 - c)
    par = y % 2
    twin = x * 4 + y + 1 - 2 * par

    def dev(pp, qq):
        xx = pp * (1 - c) + qq * c
        yy = qq * (1 - c) + pp * c
        return (z, (xx * 4 + yy) * 2 + c)

    znext = (z + 1) % nz
    zprev = (z + nz - 1) % nz
    other = chip * 2 + 1 - c

    barrier = pltpu.get_barrier_semaphore()
    peers = [dev((p + d) % 4, q) for d in (1, 2, 3)] + [dev(p, (q + d) % 4) for d in (1, 2, 3)]
    peers += [partner, (z, twin * 2 + 1 - c)]
    peers += [(znext, t), (znext, other), (zprev, t), (zprev, other)]
    for peer in peers:
        pl.semaphore_signal(barrier, inc=1, device_id=peer, device_id_type=MESH)

    sends = []

    def put(src, dst, s_sem, r_sem, device):
        cp = pltpu.make_async_remote_copy(
            src_ref=src, dst_ref=dst, send_sem=s_sem, recv_sem=r_sem, device_id=device, device_id_type=MESH
        )
        cp.start()
        sends.append(cp)

    def got(dst, s_sem, r_sem):
        pltpu.make_async_remote_copy(
            src_ref=dst, dst_ref=dst, send_sem=s_sem, recv_sem=r_sem, device_id=partner, device_id_type=MESH
        ).wait_recv()

    mycols = pl.ds(pl.multiple_of(c * 128, 128), 128)

    def local(k, src, dst):
        cp = pltpu.make_async_copy(src, dst, loc.at[k])
        cp.start()
        return cp

    cp_strm = local(0, stream, strm)
    cp_wk = local(1, wk, wkl)
    cp_wv = local(2, wv, wvl)
    cp_wq = local(3, wq, wqa.at[:, mycols])
    cp_wo = local(4, wo, woa.at[:, mycols])
    cp_inc = local(5, incoming, inc)

    zf = jnp.minimum(z, 1).astype(F32)
    cf = c.astype(F32)

    def rows(g):
        return pl.ds(pl.multiple_of(g * R + c * H, H), H)

    def other_rows(g):
        return pl.ds(pl.multiple_of(g * R + (1 - c) * H, H), H)

    def spread(tick):
        row = chosen[tick : tick + 1, :].astype(F32)
        for k in range(CAP // 128):
            lsp[tick, k * 128 : (k + 1) * 128, :] = jnp.transpose(
                jnp.broadcast_to(row[:, k * 128 : (k + 1) * 128], (128, 128))
            )

    def take_rows(tick, g, source):
        lane = lax.broadcasted_iota(jnp.int32, (R, 256), 1).astype(F32)
        pos = lsp[tick, g * R : (g + 1) * R, :]
        pos = jnp.concatenate([pos, pos], axis=1)
        total = jnp.zeros((R, 128), F32)
        for k in range(TOKENS // 256):
            hot = jnp.where(pos == lane + float(k * 256), 1.0, 0.0).astype(BF16)
            total += jnp.dot(hot, source(k), preferred_element_type=F32)
        return total

    def mine_of(value):
        low, high = value[:H], value[H:]
        return (low * (1 - cf) + high * cf).astype(BF16), (high * (1 - cf) + low * cf).astype(BF16)

    spread(0)
    cp_strm.wait()
    for g in range(N):
        mine, others = mine_of(take_rows(0, g, lambda k: strm[k * 256 : (k + 1) * 256, :]))
        gath[0, g, own, :, mycols] = mine
        pst[0, g] = others
    pl.semaphore_wait(barrier, len(peers))
    for g in range(N):
        put(pst.at[0, g], gath.at[0, g, p * 4 + q, :, mycols], pk_s.at[0, g], pk_r.at[0, g], partner)

    def gather_own(a, g):
        for k, d in enumerate((1, 3, 2)):
            put(gath.at[a, g, own], gath.at[a, g, own], ag_s.at[a, g, k], ag_r.at[a, g, k], dev((p + d) % 4, q))

    def group(qq):
        return pl.ds(qq * 4, 4)

    def gather_group(a, g):
        for k, d in enumerate((1, 3, 2)):
            got(gath.at[a, g, q * 4 + (p + 4 - d) % 4], ag_s.at[a, g, k], ag_r.at[a, g, k])
        for k, d in ((3, 1), (4, 3)):
            mine = gath.at[a, g, group(q)]
            put(mine, mine, ag_s.at[a, g, k], ag_r.at[a, g, k], dev(p, (q + d) % 4))

    def gather_far(a, g):
        before = (q + 3) % 4
        after = (q + 1) % 4
        got(gath.at[a, g, group(before)], ag_s.at[a, g, 3], ag_r.at[a, g, 3])
        half = gath.at[a, g, pl.ds(before * 4, 2)]
        put(half, half, ag_s.at[a, g, 5], ag_r.at[a, g, 5], dev(p, after))
        got(gath.at[a, g, group(after)], ag_s.at[a, g, 4], ag_r.at[a, g, 4])
        half = gath.at[a, g, pl.ds(after * 4 + 2, 2)]
        put(half, half, ag_s.at[a, g, 6], ag_r.at[a, g, 6], dev(p, before))

    def gather_end(a, g):
        far = (q + 2) % 4
        got(gath.at[a, g, pl.ds(far * 4, 2)], ag_s.at[a, g, 5], ag_r.at[a, g, 5])
        got(gath.at[a, g, pl.ds(far * 4 + 2, 2)], ag_s.at[a, g, 6], ag_r.at[a, g, 6])

    def features(qq, pp):
        return (pp * 4 + qq) * (1 - c) + (qq * 4 + pp) * c

    def project(tick, g, shift, first):
        qq = (q + shift) % 4
        query = jnp.zeros((H, 256), F32) if first else accq[g]
        keyval = jnp.zeros((H, 128), F32) if first else acck[g]
        square = jnp.zeros((H, 128), F32) if first else ssb[g]
        logit = jnp.zeros((H, 128), F32) if first else lgb[g]
        for pp in range(4):
            at = pl.ds(pl.multiple_of(features(qq, pp) * 256, 256), 256)
            wide = gath[2 * tick, g, qq * 4 + pp].astype(F32)
            scaled = (wide * gain[:, at]).astype(BF16)
            two = wide * wide
            square += two[:, :128] + two[:, 128:]
            two = scaled.astype(F32) * router[:, at].astype(F32)
            logit += two[:, :128] + two[:, 128:]
            query += jnp.dot(scaled, wqa[at, :], preferred_element_type=F32)
            keyval += jnp.dot(scaled, w2[at, :], preferred_element_type=F32)
        accq[g] = query
        acck[g] = keyval
        ssb[g] = square
        lgb[g] = logit

    def rope(value, cosine, sine):
        return value * cosine + pltpu.roll(value, 64, 1) * sine

    def project_end(tick, g):
        rstd = lax.rsqrt(jnp.sum(ssb[g], axis=1, keepdims=True) / D + 1e-05)
        kv = (acck[g] * rstd).astype(BF16)
        kvb[tick, par, rows(g), :] = kv
        part = kvb.at[tick, par, rows(g), :]
        put(part, part, kv_s.at[tick, g, 0], kv_r.at[tick, g, 0], (z, twin * 2 + c))
        put(part, part, kv_s.at[tick, g, 1], kv_r.at[tick, g, 1], (z, twin * 2 + 1 - c))
        put(part, part, kv_s.at[tick, g, 2], kv_r.at[tick, g, 2], partner)
        cosine = cosb[tick, rows(g), :]
        sine = sinb[tick, rows(g), :]
        query = accq[g] * rstd
        qs[g, :H, :] = rope(query[:, :128], cosine, sine).astype(BF16)
        qs[g, H:, :] = rope(query[:, 128:], cosine, sine).astype(BF16)
        logit = jnp.sum(lgb[g], axis=1, keepdims=True) * rstd
        slot = lax.broadcasted_iota(jnp.int32, (H, 1), 0) + (g * R + c * H)
        alive = jnp.where(slot < live[:, tick : tick + 1], 1.0, 0.0)
        mixb[g] = jnp.broadcast_to(jax.nn.sigmoid(logit) * alive, (H, 128))

    def attend(tick, g):
        got(kvb.at[tick, 1 - par, rows(g), :], kv_s.at[tick, g, 0], kv_r.at[tick, g, 0])
        got(kvb.at[tick, 1 - par, other_rows(g), :], kv_s.at[tick, g, 1], kv_r.at[tick, g, 1])
        got(kvb.at[tick, par, other_rows(g), :], kv_s.at[tick, g, 2], kv_r.at[tick, g, 2])
        span = slice(g * R, (g + 1) * R)
        low = kvb[tick, 0, span, :].astype(F32)
        high = kvb[tick, 1, span, :].astype(F32)
        left = lax.broadcasted_iota(jnp.int32, (R, 128), 1) < 64
        key = jnp.where(left, low, pltpu.roll(high, 64, 1))
        kc[span, :] = rope(key, cosb[tick, span, :], sinb[tick, span, :]).astype(BF16)
        vc[span, :] = jnp.where(left, pltpu.roll(low, 64, 1), high).astype(BF16)
        upto = (g + 1) * R
        scores = lax.dot_general(
            qs[g], kc[:upto, :], (((1,), (1,)), ((), ())), preferred_element_type=F32
        ) * (1.0 / math.sqrt(HD))
        row = lax.broadcasted_iota(jnp.int32, (2 * H, upto), 0)
        row = jnp.where(row < H, row, row - H) + (g * R + c * H)
        col = lax.broadcasted_iota(jnp.int32, (2 * H, upto), 1)
        scores = jnp.where((col <= row) & (col < live[:, tick : tick + 1]), scores, -jnp.inf)
        top = jnp.max(scores, axis=1, keepdims=True)
        weights = jnp.exp(scores - top)
        probs = (weights / jnp.sum(weights, axis=1, keepdims=True)).astype(BF16)
        result = jnp.dot(probs, vc[:upto, :], preferred_element_type=F32).astype(BF16)
        a = 2 * tick + 1
        gath[a, g, own, :, 0:128] = result[:H]
        gath[a, g, own, :, 128:256] = result[H:]
        gather_own(a, g)

    def mix_out(tick, g, shift, first):
        qq = (q + shift) % 4
        total = jnp.zeros((H, 256), F32) if first else accd[g]
        for pp in range(4):
            at = pl.ds(pl.multiple_of(features(qq, pp) * 256, 256), 256)
            total += jnp.dot(gath[2 * tick + 1, g, qq * 4 + pp], woa[at, :], preferred_element_type=F32)
        accd[g] = total

    def updated(tick, g):
        mixing = jnp.concatenate([mixb[g], mixb[g]], axis=1)
        return (gath[2 * tick, g, own].astype(F32) + mixing * accd[g]).astype(BF16)

    def finish(tick, g):
        new = updated(tick, g)
        if tick == 0:
            ub[g] = new
            put(ub.at[g], u0.at[rows(g), :], uz_s.at[g, 0], uz_r.at[g, 0], (znext, t))
            put(ub.at[g], u0.at[rows(g), :], uz_s.at[g, 1], uz_r.at[g, 1], (znext, other))
        else:
            low, high = new[:, :128].astype(F32), new[:, 128:].astype(F32)
            u1s[g] = (high * (1 - cf) + low * cf).astype(BF16)
            put(u1s.at[g], u1.at[rows(g), :], e_s.at[g], e_r.at[g], partner)
            u1[rows(g), :] = (low * (1 - cf) + high * cf).astype(BF16)

    def tables(tick):
        for g in range(CAP // 128):
            span = slice(g * 128, (g + 1) * 128)
            angle = lsp[tick, span, :] * freq[...]
            sign = jnp.where(lax.broadcasted_iota(jnp.int32, (128, 128), 1) < 64, -1.0, 1.0)
            cosb[tick, span, :] = jnp.cos(angle)
            sinb[tick, span, :] = jnp.sin(angle) * sign

    def place_kv():
        cp_wk.wait()
        cp_wv.wait()
        row = lax.broadcasted_iota(jnp.int32, (32, 128), 0)
        col = lax.broadcasted_iota(jnp.int32, (32, 128), 1)
        hot_k = jnp.where(col == row + 32 * c, 1.0, 0.0).astype(BF16)
        hot_v = jnp.where(col == row + 64 + 32 * c, 1.0, 0.0).astype(BF16)

        def some(k, _):
            at = pl.ds(pl.multiple_of(k * 512, 512), 512)
            w2o[at, :] = (
                jnp.dot(wkl[at, :], hot_k, preferred_element_type=F32)
                + jnp.dot(wvl[at, :], hot_v, preferred_element_type=F32)
            ).astype(BF16)
            return 0

        lax.fori_loop(0, D // 512, some, 0)

    def join_kv():
        got(w2p, wx_s.at[1], wx_r.at[1])

        def some(k, _):
            at = pl.ds(pl.multiple_of(k * 512, 512), 512)
            w2[at, :] = w2o[at, :] + w2p[at, :]
            return 0

        lax.fori_loop(0, D // 512, some, 0)

    for g in range(N):
        got(gath.at[0, g, own, :, mycols], pk_s.at[0, g], pk_r.at[0, g])
        gather_own(0, g)
    put(wq, wqa.at[:, mycols], wx_s.at[0], wx_r.at[0], partner)
    place_kv()
    put(w2o, w2p, wx_s.at[1], wx_r.at[1], partner)
    put(chosen, lprev, wx_s.at[3], wx_r.at[3], (znext, t))
    put(stream, bulk, wx_s.at[4], wx_r.at[4], (znext, t))
    for g in range(N):
        gather_group(0, g)
    put(wo, woa.at[:, mycols], wx_s.at[2], wx_r.at[2], partner)
    gather_far(0, 0)
    tables(0)
    gather_far(0, 1)

    def ready_weights():
        cp_wq.wait()
        got(wqa.at[:, mycols], wx_s.at[0], wx_r.at[0])
        join_kv()

    def ready_wo():
        cp_wo.wait()
        got(woa.at[:, mycols], wx_s.at[2], wx_r.at[2])

    def near(tick, g):
        project(tick, g, 0, True)
        project(tick, g, 3, False)
        project(tick, g, 1, False)

    def rest(tick, g):
        gather_end(2 * tick, g)
        project(tick, g, 2, False)
        project_end(tick, g)

    def near_out(tick, g):
        mix_out(tick, g, 0, True)
        mix_out(tick, g, 3, False)
        mix_out(tick, g, 1, False)

    def rest_out(tick, g):
        gather_end(2 * tick + 1, g)
        mix_out(tick, g, 2, False)
        finish(tick, g)

    def token_map():
        row = chosen[1:2, :].astype(F32)

        def some(k, _):
            at = pl.ds(pl.multiple_of(k * 256, 256), 256)
            token = (lax.broadcasted_iota(jnp.int32, (256, CAP), 0) + k * 256).astype(F32)
            mt[at, :] = jnp.where(token == row, 1.0, 0.0).astype(BF16)
            return 0

        lax.fori_loop(0, TOKENS // 256, some, 0)

    def base_rows():
        cp_inc.wait()
        got(bulk, wx_s.at[4], wx_r.at[4])
        got(lprev, wx_s.at[3], wx_r.at[3])

        def some(k, _):
            at = pl.ds(pl.multiple_of(k * 256, 256), 256)
            bulk_rows = bulk[at, :].astype(F32) * zf + inc[at, :].astype(F32) * (1 - zf)
            strm[at, :] = bulk_rows.astype(BF16)
            return 0

        lax.fori_loop(0, TOKENS // 256, some, 0)

    def base_take(g):
        mine, others = mine_of(take_rows(1, g, lambda k: strm[k * 256 : (k + 1) * 256, :]))
        bp[g, :, mycols] = mine
        pst[1, g] = others
        put(pst.at[1, g], bp.at[g, :, mycols], pk_s.at[1, g], pk_r.at[1, g], partner)

    def previous():
        return lprev[0:1, :].astype(F32) * zf - (1 - zf)

    ready_weights()
    near(0, 0)
    gather_far(0, 2)
    rest(0, 0)
    near(0, 1)
    gather_far(0, 3)
    rest(0, 1)
    attend(0, 0)
    near(0, 2)
    rest(0, 2)
    attend(0, 1)
    gather_group(1, 0)
    near(0, 3)
    rest(0, 3)
    attend(0, 2)
    gather_group(1, 1)
    gather_far(1, 0)
    attend(0, 3)
    gather_group(1, 2)
    gather_far(1, 1)
    ready_wo()
    near_out(0, 0)
    gather_group(1, 3)
    gather_far(1, 2)
    rest_out(0, 0)
    near_out(0, 1)
    gather_far(1, 3)
    rest_out(0, 1)
    spread(1)
    base_rows()
    for g in range(N):
        base_take(g)
    near_out(0, 2)
    rest_out(0, 2)
    near_out(0, 3)
    rest_out(0, 3)
    tables(1)
    token_map()

    for g in range(N):
        got(bp.at[g, :, mycols], pk_s.at[1, g], pk_r.at[1, g])
    for g in range(N):
        got(u0.at[rows(g), :], uz_s.at[g, 0], uz_r.at[g, 0])
        got(u0.at[other_rows(g), :], uz_s.at[g, 1], uz_r.at[g, 1])
    for g in range(N):
        pos = lsp[1, rows(g), :]
        pos = jnp.concatenate([pos] * (CAP // 128), axis=1)
        same = jnp.where(pos == previous(), 1.0, 0.0)
        kept = 1.0 - jnp.sum(same, axis=1, keepdims=True)
        moved = jnp.dot(same.astype(BF16), u0[...], preferred_element_type=F32)
        gath[2, g, own] = (bp[g].astype(F32) * kept + moved).astype(BF16)
        gather_own(2, g)

    def unlisted():
        mine = u0[:, mycols]
        both = jnp.concatenate([mine, jnp.ones((CAP, 128), BF16)], axis=1)
        row = previous()

        def some(k, _):
            at = pl.ds(pl.multiple_of(k * 256, 256), 256)
            token = (lax.broadcasted_iota(jnp.int32, (256, CAP), 0) + k * 256).astype(F32)
            hot = jnp.where(token == row, 1.0, 0.0).astype(BF16)
            moved = jnp.dot(hot, both, preferred_element_type=F32)
            listed = jnp.dot(mt[at, :], jnp.ones((CAP, 128), BF16), preferred_element_type=F32)
            state = strm[at, :].astype(F32) * (1.0 - moved[:, 128:]) + moved[:, :128]
            facc[at, :] = state * (1.0 - listed)
            return 0

        lax.fori_loop(0, TOKENS // 256, some, 0)

    for g in range(N):
        gather_group(2, g)
    unlisted()
    gather_far(2, 0)
    gather_far(2, 1)
    near(1, 0)
    gather_far(2, 2)
    rest(1, 0)
    near(1, 1)
    gather_far(2, 3)
    rest(1, 1)
    attend(1, 0)
    near(1, 2)
    rest(1, 2)
    attend(1, 1)
    gather_group(3, 0)
    near(1, 3)
    rest(1, 3)
    attend(1, 2)
    gather_group(3, 1)
    gather_far(3, 0)
    attend(1, 3)
    gather_group(3, 2)
    gather_far(3, 1)
    near_out(1, 0)
    gather_group(3, 3)
    gather_far(3, 2)
    rest_out(1, 0)
    near_out(1, 1)
    gather_far(3, 3)
    rest_out(1, 1)
    near_out(1, 2)
    rest_out(1, 2)
    near_out(1, 3)
    rest_out(1, 3)
    for g in range(N):
        got(u1.at[other_rows(g), :], e_s.at[g], e_r.at[g])

    def write(k, _):
        at = pl.ds(pl.multiple_of(k * 256, 256), 256)
        new = jnp.dot(mt[at, :], u1[...], preferred_element_type=F32)
        out[at, :] = (facc[at, :] + new).astype(BF16)
        return 0

    lax.fori_loop(0, TOKENS // 256, write, 0)
    for cp in sends:
        cp.wait_send()


def body(stream, incoming, chosen, live, norm_gain, router, wq, wk, wv, wo):
    half = HD // 2
    freq = np.exp(-math.log(500000.0) * 2.0 * np.arange(half) / HD)
    freq = jnp.asarray(np.concatenate([freq, freq])[None, :], F32)
    vmem = pl.BlockSpec(memory_space=pltpu.VMEM)
    hbm = pl.BlockSpec(memory_space=pl.ANY)
    dma = pltpu.SemaphoreType.DMA
    scratch = [
        pltpu.VMEM((TOKENS, 128), BF16),
        pltpu.VMEM((TOKENS, 128), BF16),
        pltpu.VMEM((TOKENS, 128), BF16),
        pltpu.VMEM((D, 256), BF16),
        pltpu.VMEM((D, 256), BF16),
        pltpu.VMEM((D, 32), BF16),
        pltpu.VMEM((D, 32), BF16),
        pltpu.VMEM((D, 128), BF16),
        pltpu.VMEM((D, 128), BF16),
        pltpu.VMEM((D, 128), BF16),
        pltpu.VMEM((2, CAP), jnp.int32),
        pltpu.VMEM((2, CAP, 128), F32),
        pltpu.VMEM((2, CAP, 128), F32),
        pltpu.VMEM((2, CAP, 128), F32),
        pltpu.VMEM((4, N, 16, H, 256), BF16),
        pltpu.VMEM((2, N, H, 128), BF16),
        pltpu.VMEM((N, H, 256), BF16),
        pltpu.VMEM((2, 2, CAP, 128), BF16),
        pltpu.VMEM((CAP, 128), BF16),
        pltpu.VMEM((CAP, 128), BF16),
        pltpu.VMEM((N, 2 * H, 128), BF16),
        pltpu.VMEM((N, H, 256), F32),
        pltpu.VMEM((N, H, 128), F32),
        pltpu.VMEM((N, H, 128), F32),
        pltpu.VMEM((N, H, 128), F32),
        pltpu.VMEM((N, H, 128), F32),
        pltpu.VMEM((N, H, 256), F32),
        pltpu.VMEM((N, H, 256), BF16),
        pltpu.VMEM((CAP, 256), BF16),
        pltpu.VMEM((N, H, 128), BF16),
        pltpu.VMEM((CAP, 128), BF16),
        pltpu.VMEM((TOKENS, CAP), BF16),
        pltpu.VMEM((TOKENS, 128), F32),
        dma((6,)),
        dma((4, N, 7)),
        dma((4, N, 7)),
        dma((2, N)),
        dma((2, N)),
        dma((2, N, 3)),
        dma((2, N, 3)),
        dma((N, 2)),
        dma((N, 2)),
        dma((5,)),
        dma((5,)),
        dma((N,)),
        dma((N,)),
    ]
    result = pl.pallas_call(
        kernel,
        out_shape=jax.ShapeDtypeStruct((TOKENS, 128), BF16),
        in_specs=[hbm, hbm, vmem, vmem, vmem, vmem, vmem, hbm, hbm, hbm, hbm],
        out_specs=vmem,
        scratch_shapes=scratch,
        compiler_params=pltpu.CompilerParams(
            collective_id=0, has_side_effects=True, vmem_limit_bytes=48 * 2**20
        ),
        name="relay",
    )(stream[0], incoming[0], chosen[0], live, norm_gain, router, freq, wq[0], wk[0], wv[0], wo[0])
    return result[None]


def solution(mesh):
    in_specs = (
        P("pipe", None, "tp"),
        P(None, None, "tp"),
        P("pipe", None, None),
        P("pipe", None),
        P("pipe", None),
        P("pipe", None),
        P("pipe", None, "tp"),
        P("pipe", None, "tp"),
        P("pipe", None, "tp"),
        P("pipe", None, "tp"),
    )
    out_specs = P("pipe", None, "tp")
    return jax.shard_map(body, mesh=mesh, in_specs=in_specs, out_specs=out_specs, check_vma=False)
```

time: 348 us -> 110 us (0.32)
  waiting for transfers between devices: 276 us -> 0 us
  Pallas kernels: 0 us -> 102 us
  matrix products: 22.8 us -> 0 us
  between operations: 13.5 us -> 0.08 us
  starting transfers between devices: 13.4 us -> 0 us
  other arithmetic: 12.5 us -> 0 us
    all_gather x4 -> x0, waiting for transfers between devices: 260 us -> none  [the longest x2 136 us: project_rows(): gathered = lax.all_gather(picked, 'tp', axis=1, tiled=True)]
    pallas_call x0 -> x1, Pallas kernels: none -> 102 us  [body(): pl.pallas_call(kernel, out_shape=jax.ShapeDtypeStruct((TOKENS, 128), BF16...]
    dot_general x14 -> x0, matrix products: 22.8 us -> none  [the longest x2 6.95 us: routed_block(): jnp.dot(lax.all_gather(attended, 'tp', axis=1, tiled=True), w_out, prefer...]
    ppermute x5 -> x0, waiting for transfers between devices: 16.5 us -> none  [the longest x1 11 us: from_behind(): return lax.ppermute(block, axis, route)]
    ppermute x5 -> x0, starting transfers between devices: 13.1 us -> none  [the longest x4 9.84 us: from_partner(): return lax.ppermute(value, axis, pairs)]
    unnamed x29 -> x23, local copies, waits for them, and re-layouts: 2.18 us -> 6.78 us
    reduce_sum x4 -> x0, other arithmetic: 4.53 us -> none  [the longest x2 4.13 us: project_rows(): square_sum = jnp.sum(widened * widened, axis=1)]
  transfers between devices with their start and end apart: 9 -> 0, of which waited for: 9 -> 0; matrix products, arithmetic and copies ran while one was open for 2% -> 0% of each run, Pallas kernels for 0% -> 0%
where the time goes in v1:
time: 110 us; the launch traced here: 109 us
  Pallas kernels  102 us (93%)
  local copies, waits for them, and re-layouts  6.78 us (6%)
    pallas_call x1, Pallas kernels, body(): pl.pallas_call(kernel, out_shape=jax.ShapeDtypeStruct((TOKENS, 128), BF16...  102 us
    unnamed x23, local copies, waits for them, and re-layouts  6.78 us

profile of v1, /device:TPU:1, one launch (start us, length us, event | category | flops | bytes accessed | tf_op | source)
XLA Modules:
  0.0 109.3 jit_solution(18146150835470672619)
XLA Ops:
  0.0 0.0 copy-start.9
  0.0 0.0 copy-start
  0.0 1.5 %copy.12 = bf16[1,4096,32]{2,1,0:T(8,128)(2,1)S(1)} copy(bf16[1,4096,32]{1,2,0:T(8,128)(2,1)} %param.18) | data formatting | bytes 524288 | tf_op args[7]
  1.5 0.0 copy-done.9
  1.5 0.0 copy-start.4
  1.6 0.0 copy-start.5
  1.6 0.0 copy-start.6
  1.6 0.5 copy.13
  2.1 0.0 copy-start.7
  2.1 0.0 copy-start.8
  2.1 0.0 copy-done
  2.1 0.2 copy-done.4
  2.3 0.0 copy-done.5
  2.3 0.0 copy-done.6
  2.3 0.4 copy-done.7
  2.7 0.0 copy-done.8
  2.7 0.0 copy-start.1
  2.7 1.2 %copy-done.1 = bf16[1,4096,128]{2,1,0:T(8,128)(2,1)S(1)} copy-done((bf16[1,4096,128]{2,1,0:T(8,128)(2,1)S(1)}, bf16[1,4096,128]{2,1,0:T(8,128)(2,1)}, u32[]{:S(2)}) %copy-start.1) | copy-done | bytes 1048600
  4.0 0.0 copy-start.2
  4.0 1.0 copy-done.2
  5.0 0.0 copy-start.3
  5.0 1.0 copy-done.3
  6.1 102.4 %relay.1 = bf16[2048,128]{1,0:T(8,128)(2,1)S(1)} custom-call(bf16[2048,128]{1,0:T(8,128)(2,1)S(1)} %bitcast.13, bf16[2048,128]{1,0:T(8,128)(2,1)S(1)} %bitcast.14, s32[2,512]{1,0:T(2,128)S(1)} %bitcast.15, s32[1,2]{1,0:T(1,128)S(1)} %copy-done.7, f32[1,4096]{1,0:T(1,128)S(1)} %copy-done.4, bf16[1,4096]{1,0:T(2,128)(2,1)S(1)} %copy-done.5, ...), custom_call_target="tpu_custom_call" | custom-call | tf_op jit(solution)/shard_map/relay/pallas_call | solution.py:542
  108.5 0.8 copy.15
Async XLA Ops:
  0.0 1.5 %copy-start.9 = (bf16[1,4096,32]{1,2,0:T(8,128)(2,1)S(1)}, bf16[1,4096,32]{1,2,0:T(8,128)(2,1)}, u32[]{:S(2)}) copy-start(bf16[1,4096,32]{1,2,0:T(8,128)(2,1)} %param.19) | copy-start | bytes 786436
  0.0 2.1 %copy-start = (bf16[1,4096,128]{2,1,0:T(8,128)(2,1)S(1)}, bf16[1,4096,128]{2,1,0:T(8,128)(2,1)}, u32[]{:S(2)}) copy-start(bf16[1,4096,128]{2,1,0:T(8,128)(2,1)} %param.17) | copy-start | bytes 3145732
  1.5 0.7 copy-start.4
  1.6 0.7 copy-start.5
  1.6 0.7 copy-start.6
  2.1 0.7 copy-start.7
  2.1 0.7 copy-start.8
  2.7 1.2 %copy-start.1 = (bf16[1,4096,128]{2,1,0:T(8,128)(2,1)S(1)}, bf16[1,4096,128]{2,1,0:T(8,128)(2,1)}, u32[]{:S(2)}) copy-start(bf16[1,4096,128]{2,1,0:T(8,128)(2,1)} %param.20) | copy-start | bytes 3145732
  4.0 1.0 copy-start.2
  5.0 1.0 copy-start.3

commit v2 on v1

v2 whole, which is shorter than its diff:
```python
import functools
import math

import jax
import jax.numpy as jnp
import numpy as np
from jax import lax
from jax.experimental import pallas as pl
from jax.experimental.pallas import tpu as pltpu
from jax.sharding import PartitionSpec as P

MESH = pl.DeviceIdType.MESH
F32 = jnp.float32
BF16 = jnp.bfloat16

D = 4096
TOKENS = 2048
CAP = 512
HD = 128
N = 2
R = CAP // N
H = R // 2


def kernel(
    stream, incoming, chosen, live, gain, router, freq, wq, wk, wv, wo, out,
    strm, inc, bulk, wall, woa, wod, wkl, wvl, w2o, w2p, gains, routes, same, lprev, lsp, cosb, sinb, gath, att, rss, rsr, pst, bp, kvb, kc, vc,
    qs, accp, ssb, lgb, mixb, accd, ub, accm, u0, u1s, u1, mt, facc,
    loc, ag_s, ag_r, at_s, at_r, rs_s, rs_r, wo_s, wo_r, pk_s, pk_r, kv_s, kv_r, uz_s, uz_r, wx_s, wx_r, e_s, e_r,
):
    z = lax.axis_index("pipe")
    t = lax.axis_index("tp")
    nz = lax.axis_size("pipe")
    c = t % 2
    chip = t // 2
    y = chip % 4
    x = chip // 4
    p = x * (1 - c) + y * c
    q = y * (1 - c) + x * c
    own = q * 4 + p
    partner = (z, chip * 2 + 1 - c)
    par = y % 2
    twin = x * 4 + y + 1 - 2 * par

    def dev(pp, qq):
        xx = pp * (1 - c) + qq * c
        yy = qq * (1 - c) + pp * c
        return (z, (xx * 4 + yy) * 2 + c)

    def cross(pp, qq):
        xx = pp * (1 - c) + qq * c
        yy = qq * (1 - c) + pp * c
        return (z, (xx * 4 + yy) * 2 + 1 - c)

    znext = (z + 1) % nz
    zprev = (z + nz - 1) % nz
    other = chip * 2 + 1 - c

    barrier = pltpu.get_barrier_semaphore()
    peers = [dev((p + d) % 4, q) for d in (1, 2, 3)] + [dev(p, (q + d) % 4) for d in (1, 2, 3)]
    peers += [cross((p + d) % 4, q) for d in (1, 2, 3)] + [cross(p, (q + d) % 4) for d in (1, 2, 3)] + [partner]
    peers += [(znext, t), (znext, other), (zprev, t), (zprev, other)]
    for peer in peers:
        pl.semaphore_signal(barrier, inc=1, device_id=peer, device_id_type=MESH)

    sends = []

    def put(src, dst, s_sem, r_sem, device):
        cp = pltpu.make_async_remote_copy(
            src_ref=src, dst_ref=dst, send_sem=s_sem, recv_sem=r_sem, device_id=device, device_id_type=MESH
        )
        cp.start()
        sends.append(cp)

    def got(dst, s_sem, r_sem):
        pltpu.make_async_remote_copy(
            src_ref=dst, dst_ref=dst, send_sem=s_sem, recv_sem=r_sem, device_id=partner, device_id_type=MESH
        ).wait_recv()

    mycols = pl.ds(pl.multiple_of(c * 128, 128), 128)

    def local(k, src, dst):
        cp = pltpu.make_async_copy(src, dst, loc.at[k])
        cp.start()
        return cp

    cp_strm = local(0, stream, strm)
    cp_wk = local(1, wk, wkl)
    cp_wv = local(2, wv, wvl)
    cp_inc = local(5, incoming, inc)

    def slot_of(k, cc):
        return ((k % 4) * 4 + k // 4) * (1 - cc) + k * cc

    def part(k):
        return pl.ds(pl.multiple_of(k * 256, 256), 256)

    def lay_out(source, target, sem):
        def some(k, _):
            pltpu.make_async_copy(source.at[part(k), :], target.at[part(slot_of(k, c)), mycols], sem).start()
            return 0

        lax.fori_loop(0, 16, some, 0)

    lay_out(wq, wall, loc.at[3])

    def put_out(source, target, columns, k):
        def some(i, _):
            pltpu.make_async_remote_copy(
                src_ref=source.at[part(i), :], dst_ref=target.at[part(slot_of(i, 1 - c)), columns],
                send_sem=wx_s.at[k], recv_sem=wx_r.at[k], device_id=partner, device_id_type=MESH,
            ).start()
            return 0

        lax.fori_loop(0, 16, some, 0)
        whole = target.at[:, columns]
        sends.append(
            pltpu.make_async_remote_copy(
                src_ref=whole, dst_ref=whole, send_sem=wx_s.at[k], recv_sem=wx_r.at[k],
                device_id=partner, device_id_type=MESH,
            )
        )

    def chip_of(pp, qq, cc):
        return (pp * 4 + qq) * (1 - cc) + (qq * 4 + pp) * cc

    def out_weights(d):
        qq = (q + d) % 4
        pp = (p + d) % 4
        for k in range(4):
            if d == 0:
                pltpu.make_async_copy(wo.at[part(chip_of(k, qq, c)), :], wod.at[q, k, :, mycols], loc.at[6]).start()
            else:
                pltpu.make_async_remote_copy(
                    src_ref=wo.at[part(chip_of(k, qq, c)), :], dst_ref=wod.at[q, k, :, mycols],
                    send_sem=wo_s.at[d, 0], recv_sem=wo_r.at[d, 0], device_id=dev(p, qq), device_id_type=MESH,
                ).start()
            pltpu.make_async_remote_copy(
                src_ref=wo.at[part(chip_of(k, pp, 1 - c)), :], dst_ref=wod.at[p, k, :, mycols],
                send_sem=wo_s.at[d, 1], recv_sem=wo_r.at[d, 1], device_id=cross(pp, q), device_id_type=MESH,
            ).start()
        for way in range(2):
            if d or way:
                whole = wod.at[0, :, :, mycols]
                sends.append(
                    pltpu.make_async_remote_copy(
                        src_ref=whole, dst_ref=whole, send_sem=wo_s.at[d, way], recv_sem=wo_r.at[d, way],
                        device_id=partner, device_id_type=MESH,
                    )
                )

    theircols = pl.ds(pl.multiple_of((1 - c) * 128, 128), 128)
    zf = jnp.minimum(z, 1).astype(F32)
    cf = c.astype(F32)

    def rows(g):
        return pl.ds(pl.multiple_of(g * R + c * H, H), H)

    def other_rows(g):
        return pl.ds(pl.multiple_of(g * R + (1 - c) * H, H), H)

    def spread(tick):
        row = chosen[tick : tick + 1, :].astype(F32)
        for k in range(CAP // 128):
            lsp[tick, k * 128 : (k + 1) * 128, :] = jnp.transpose(
                jnp.broadcast_to(row[:, k * 128 : (k + 1) * 128], (128, 128))
            )

    def take_rows(tick, g, source):
        lane = lax.broadcasted_iota(jnp.int32, (R, 256), 1).astype(F32)
        pos = lsp[tick, g * R : (g + 1) * R, :]
        pos = jnp.concatenate([pos, pos], axis=1)
        total = jnp.zeros((R, 128), F32)
        for k in range(TOKENS // 256):
            hot = jnp.where(pos == lane + float(k * 256), 1.0, 0.0).astype(BF16)
            total += jnp.dot(hot, source(k), preferred_element_type=F32)
        return total

    def mine_of(value):
        low, high = value[:H], value[H:]
        return (low * (1 - cf) + high * cf).astype(BF16), (high * (1 - cf) + low * cf).astype(BF16)

    def gather_own(a, g):
        for k, d in enumerate((1, 3, 2)):
            put(gath.at[a, g, own], gath.at[a, g, own], ag_s.at[a, g, k], ag_r.at[a, g, k], dev((p + d) % 4, q))

    def group(qq):
        return pl.ds(qq * 4, 4)

    def gather_group(a, g):
        for k, d in enumerate((1, 3, 2)):
            got(gath.at[a, g, q * 4 + (p + 4 - d) % 4], ag_s.at[a, g, k], ag_r.at[a, g, k])
        for k, d in ((3, 1), (4, 3)):
            mine = gath.at[a, g, group(q)]
            put(mine, mine, ag_s.at[a, g, k], ag_r.at[a, g, k], dev(p, (q + d) % 4))

    def gather_far(a, g):
        before = (q + 3) % 4
        after = (q + 1) % 4
        got(gath.at[a, g, group(before)], ag_s.at[a, g, 3], ag_r.at[a, g, 3])
        half = gath.at[a, g, pl.ds(before * 4, 2)]
        put(half, half, ag_s.at[a, g, 5], ag_r.at[a, g, 5], dev(p, after))
        got(gath.at[a, g, group(after)], ag_s.at[a, g, 4], ag_r.at[a, g, 4])
        half = gath.at[a, g, pl.ds(after * 4 + 2, 2)]
        put(half, half, ag_s.at[a, g, 6], ag_r.at[a, g, 6], dev(p, before))

    def gather_end(a, g):
        far = (q + 2) % 4
        got(gath.at[a, g, pl.ds(far * 4, 2)], ag_s.at[a, g, 5], ag_r.at[a, g, 5])
        got(gath.at[a, g, pl.ds(far * 4 + 2, 2)], ag_s.at[a, g, 6], ag_r.at[a, g, 6])

    def features(slot):
        return ((slot % 4) * 4 + slot // 4) * (1 - c) + slot * c

    def order_vectors():
        for k in range(16):
            at = part(features(k))
            gains[:, k * 256 : (k + 1) * 256] = gain[:, at]
            routes[:, k * 256 : (k + 1) * 256] = router[:, at].astype(F32)

    def project(tick, g, shifts, first):
        sums = jnp.zeros((H, 384), F32) if first else accp[g]
        square = jnp.zeros((H, 128), F32) if first else ssb[g]
        logit = jnp.zeros((H, 128), F32) if first else lgb[g]
        for shift in shifts:
            qq = (q + shift) % 4
            for pp in range(4):
                slot = qq * 4 + pp
                wide = gath[2 * tick, g, slot].astype(F32)
                scaled = (wide * gains[:, part(slot)]).astype(BF16)
                two = wide * wide
                square += two[:, :128] + two[:, 128:]
                two = scaled.astype(F32) * routes[:, part(slot)]
                logit += two[:, :128] + two[:, 128:]
                sums += jnp.dot(scaled, wall[part(slot), :], preferred_element_type=F32)
        return sums, square, logit

    def near(tick, g):
        accp[g], ssb[g], lgb[g] = project(tick, g, (0, 3, 1), True)

    def rope(value, cosine, sine):
        return value * cosine + pltpu.roll(value, 64, 1) * sine

    def rest(tick, g):
        gather_end(2 * tick, g)
        sums, square, logit = project(tick, g, (2,), False)
        rstd = lax.rsqrt(jnp.sum(square, axis=1, keepdims=True) / D + 1e-05)
        kv = (sums[:, 256:] * rstd).astype(BF16)
        kvb[tick, par, rows(g), :] = kv
        mine = kvb.at[tick, par, rows(g), :]
        put(mine, mine, kv_s.at[tick, g, 0], kv_r.at[tick, g, 0], (z, twin * 2 + c))
        put(mine, mine, kv_s.at[tick, g, 1], kv_r.at[tick, g, 1], (z, twin * 2 + 1 - c))
        put(mine, mine, kv_s.at[tick, g, 2], kv_r.at[tick, g, 2], partner)
        cosine = cosb[tick, rows(g), :]
        sine = sinb[tick, rows(g), :]
        query = sums * rstd
        qs[g, :H, :] = rope(query[:, :128], cosine, sine).astype(BF16)
        qs[g, H:, :] = rope(query[:, 128:256], cosine, sine).astype(BF16)
        logit = jnp.sum(logit, axis=1, keepdims=True) * rstd
        slot = lax.broadcasted_iota(jnp.int32, (H, 1), 0) + (g * R + c * H)
        alive = jnp.where(slot < live[:, tick : tick + 1], 1.0, 0.0)
        mixb[g] = jnp.broadcast_to(jax.nn.sigmoid(logit) * alive, (H, 128))

    def attend(tick, g):
        got(kvb.at[tick, 1 - par, rows(g), :], kv_s.at[tick, g, 0], kv_r.at[tick, g, 0])
        got(kvb.at[tick, 1 - par, other_rows(g), :], kv_s.at[tick, g, 1], kv_r.at[tick, g, 1])
        got(kvb.at[tick, par, other_rows(g), :], kv_s.at[tick, g, 2], kv_r.at[tick, g, 2])
        span = slice(g * R, (g + 1) * R)
        low = kvb[tick, 0, span, :].astype(F32)
        high = kvb[tick, 1, span, :].astype(F32)
        left = lax.broadcasted_iota(jnp.int32, (R, 128), 1) < 64
        key = jnp.where(left, low, pltpu.roll(high, 64, 1))
        kc[span, :] = rope(key, cosb[tick, span, :], sinb[tick, span, :]).astype(BF16)
        vc[span, :] = jnp.where(left, pltpu.roll(low, 64, 1), high).astype(BF16)
        upto = (g + 1) * R
        scores = lax.dot_general(
            qs[g], kc[:upto, :], (((1,), (1,)), ((), ())), preferred_element_type=F32
        ) * (1.0 / math.sqrt(HD))
        row = lax.broadcasted_iota(jnp.int32, (2 * H, upto), 0)
        row = jnp.where(row < H, row, row - H) + (g * R + c * H)
        col = lax.broadcasted_iota(jnp.int32, (2 * H, upto), 1)
        scores = jnp.where((col <= row) & (col < live[:, tick : tick + 1]), scores, -jnp.inf)
        top = jnp.max(scores, axis=1, keepdims=True)
        weights = jnp.exp(scores - top)
        probs = (weights / jnp.sum(weights, axis=1, keepdims=True)).astype(BF16)
        result = jnp.dot(probs, vc[:upto, :], preferred_element_type=F32).astype(BF16)
        if tick == 0:
            gath[1, g, own, :, 0:128] = result[:H]
            gath[1, g, own, :, 128:256] = result[H:]
            gather_own(1, g)
        else:
            att[g, p, :, 0:128] = result[:H]
            att[g, p, :, 128:256] = result[H:]
            mine = att.at[g, p]
            for k, d in enumerate((1, 3, 2)):
                put(mine, mine, at_s.at[g, k], at_r.at[g, k], dev((p + d) % 4, q))

    def out_part(g, shifts, first):
        total = jnp.zeros((H, 256), F32) if first else accd[g]
        for shift in shifts:
            qq = (q + shift) % 4
            for pp in range(4):
                slot = qq * 4 + pp
                total += jnp.dot(gath[1, g, slot], woa[part(slot), :], preferred_element_type=F32)
        return total

    def near_out(tick, g):
        accd[g] = out_part(g, (0, 3, 1), True)

    def mix_out(tick, g):
        for k, d in enumerate((1, 3, 2)):
            got(att.at[g, (p + 4 - d) % 4], at_s.at[g, k], at_r.at[g, k])
        for d in (2, 1, 3, 0):
            qq = (q + d) % 4
            total = jnp.zeros((H, 256), F32)
            for pp in range(4):
                total += jnp.dot(att[g, pp], wod[qq, pp], preferred_element_type=F32)
            if d == 0:
                accd[g] = total
            else:
                rss[g, d - 1] = total.astype(BF16)
                put(
                    rss.at[g, d - 1], rsr.at[g, d - 1], rs_s.at[g, d - 1], rs_r.at[g, d - 1],
                    dev(p, qq),
                )

    def rest_out(tick, g):
        gather_end(2 * tick + 1, g)
        delta = out_part(g, (2,), False)
        update(tick, g, delta)

    def finish(tick, g):
        delta = accd[g]
        for d in (1, 3, 2):
            got(rsr.at[g, d - 1], rs_s.at[g, d - 1], rs_r.at[g, d - 1])
            delta += rsr[g, d - 1].astype(F32)
        update(tick, g, delta)

    def update(tick, g, delta):
        mixing = jnp.concatenate([mixb[g], mixb[g]], axis=1)
        new = (gath[2 * tick, g, own].astype(F32) + mixing * delta).astype(BF16)
        if tick == 0:
            ub[g] = new
            put(ub.at[g], u0.at[rows(g), :], uz_s.at[g, 0], uz_r.at[g, 0], (znext, t))
            put(ub.at[g], u0.at[rows(g), :], uz_s.at[g, 1], uz_r.at[g, 1], (znext, other))
        else:
            low, high = new[:, :128].astype(F32), new[:, 128:].astype(F32)
            u1s[g] = (high * (1 - cf) + low * cf).astype(BF16)
            put(u1s.at[g], u1.at[rows(g), :], e_s.at[g], e_r.at[g], partner)
            u1[rows(g), :] = (low * (1 - cf) + high * cf).astype(BF16)

    def tables(tick):
        for g in range(CAP // 128):
            span = slice(g * 128, (g + 1) * 128)
            angle = lsp[tick, span, :] * freq[...]
            sign = jnp.where(lax.broadcasted_iota(jnp.int32, (128, 128), 1) < 64, -1.0, 1.0)
            cosb[tick, span, :] = jnp.cos(angle)
            sinb[tick, span, :] = jnp.sin(angle) * sign

    def place_kv():
        cp_wk.wait()
        cp_wv.wait()
        row = lax.broadcasted_iota(jnp.int32, (64, 128), 0)
        col = lax.broadcasted_iota(jnp.int32, (64, 128), 1)
        row = jnp.where(row < 32, row, row + 32) + 32 * c
        hot = jnp.where(col == row, 1.0, 0.0).astype(BF16)

        def some(k, _):
            at = pl.ds(pl.multiple_of(k * 512, 512), 512)
            both = jnp.concatenate([wkl[:, at], wvl[:, at]], axis=0)
            w2o[at, :] = lax.dot_general(both, hot, (((0,), (0,)), ((), ())), preferred_element_type=F32).astype(BF16)
            return 0

        lax.fori_loop(0, D // 512, some, 0)

    def ready_weights():
        pltpu.make_async_copy(wq, wall.at[:, mycols], loc.at[3]).wait()
        got(wall.at[:, theircols], wx_s.at[0], wx_r.at[0])
        got(w2p, wx_s.at[1], wx_r.at[1])

        def some(k, _):
            wall[part(k), 256:] = w2o[part(features(k)), :] + w2p[part(k), :]
            return 0

        lax.fori_loop(0, 16, some, 0)

    def ready_wo():
        pltpu.make_async_copy(wo, woa.at[:, mycols], loc.at[4]).wait()
        got(woa.at[:, theircols], wx_s.at[2], wx_r.at[2])

    def ready_ring():
        pltpu.make_async_copy(wod.at[q, :, :, mycols], wod.at[q, :, :, mycols], loc.at[6]).wait()
        got(wod.at[q, :, :, theircols], wo_s.at[0, 1], wo_r.at[0, 1])
        for d in (1, 3, 2):
            from_q = (q + 4 - d) % 4
            got(wod.at[from_q, :, :, mycols], wo_s.at[d, 0], wo_r.at[d, 0])
            got(wod.at[from_q, :, :, theircols], wo_s.at[d, 1], wo_r.at[d, 1])

    def token_map():
        row = chosen[1:2, :].astype(F32)

        def some(k, _):
            token = (lax.broadcasted_iota(jnp.int32, (256, CAP), 0) + k * 256).astype(F32)
            hot = jnp.where(token == row, 1.0, 0.0).astype(BF16)
            mt[part(k), :] = hot
            facc[part(k), :] = 1.0 - jnp.dot(hot, jnp.ones((CAP, 128), BF16), preferred_element_type=F32)
            return 0

        lax.fori_loop(0, TOKENS // 256, some, 0)

    def base_rows():
        cp_inc.wait()
        got(bulk, wx_s.at[4], wx_r.at[4])
        got(lprev, wx_s.at[3], wx_r.at[3])

        def some(k, _):
            mixed = bulk[part(k), :].astype(F32) * zf + inc[part(k), :].astype(F32) * (1 - zf)
            strm[part(k), :] = mixed.astype(BF16)
            return 0

        lax.fori_loop(0, TOKENS // 256, some, 0)

    def base_take(g):
        mine, others = mine_of(take_rows(1, g, lambda k: strm[k * 256 : (k + 1) * 256, :]))
        bp[g, :, mycols] = mine
        pst[1, g] = others
        put(pst.at[1, g], bp.at[g, :, mycols], pk_s.at[1, g], pk_r.at[1, g], partner)

    def previous():
        return lprev[0:1, :].astype(F32) * zf - (1 - zf)

    def base_kept(g):
        got(bp.at[g, :, theircols], pk_s.at[1, g], pk_r.at[1, g])
        pos = lsp[1, rows(g), :]
        pos = jnp.concatenate([pos] * (CAP // 128), axis=1)
        hot = jnp.where(pos == previous(), 1.0, 0.0)
        same[g * H : (g + 1) * H, :] = hot.astype(BF16)
        accm[g * H : (g + 1) * H, :] = bp[g].astype(F32) * (1.0 - jnp.sum(hot, axis=1, keepdims=True))

    def base_moved(g):
        got(u0.at[rows(g), :], uz_s.at[g, 0], uz_r.at[g, 0])
        got(u0.at[other_rows(g), :], uz_s.at[g, 1], uz_r.at[g, 1])
        span = slice(g * R, (g + 1) * R)
        total = accm[...] + jnp.dot(same[:, span], u0[span, :], preferred_element_type=F32)
        if g < N - 1:
            accm[...] = total
        else:
            for k in range(N):
                gath[2, k, own] = total[k * H : (k + 1) * H].astype(BF16)
                gather_own(2, k)

    def unlisted(first, last):
        both = jnp.concatenate([u0[:, mycols], jnp.ones((CAP, 128), BF16)], axis=1)
        row = previous()

        def some(k, _):
            token = (lax.broadcasted_iota(jnp.int32, (256, CAP), 0) + k * 256).astype(F32)
            hot = jnp.where(token == row, 1.0, 0.0).astype(BF16)
            moved = jnp.dot(hot, both, preferred_element_type=F32)
            state = strm[part(k), :].astype(F32) * (1.0 - moved[:, 128:]) + moved[:, :128]
            facc[part(k), :] = state * facc[part(k), :]
            return 0

        lax.fori_loop(first, last, some, 0)

    def write(g):
        got(u1.at[other_rows(g), :], e_s.at[g], e_r.at[g])
        span = slice(g * R, (g + 1) * R)

        def some(k, _):
            total = facc[part(k), :] + jnp.dot(mt[part(k), span], u1[span, :], preferred_element_type=F32)
            if g < N - 1:
                facc[part(k), :] = total
            else:
                out[part(k), :] = total.astype(BF16)
            return 0

        lax.fori_loop(0, TOKENS // 256, some, 0)

    def pick(g):
        mine, others = mine_of(take_rows(0, g, lambda k: strm[k * 256 : (k + 1) * 256, :]))
        gath[0, g, own, :, mycols] = mine
        pst[0, g] = others

    def swap(g):
        put(pst.at[0, g], gath.at[0, g, p * 4 + q, :, mycols], pk_s.at[0, g], pk_r.at[0, g], partner)

    def swapped(g):
        got(gath.at[0, g, own, :, theircols], pk_s.at[0, g], pk_r.at[0, g])

    spread(0)
    cp_strm.wait()
    pick(0)
    pl.semaphore_wait(barrier, len(peers))
    swap(0)
    pick(1)
    swap(1)
    swapped(0)
    gather_own(0, 0)
    swapped(1)
    gather_own(0, 1)
    put_out(wq, wall, mycols, 0)
    put(chosen, lprev, wx_s.at[3], wx_r.at[3], (znext, t))
    put(stream, bulk, wx_s.at[4], wx_r.at[4], (znext, t))
    order_vectors()
    gather_group(0, 0)
    gather_group(0, 1)
    place_kv()
    put_out(w2o, w2p, slice(None), 1)
    gather_far(0, 0)
    lay_out(wo, woa, loc.at[4])
    put_out(wo, woa, mycols, 2)
    tables(0)
    gather_far(0, 1)
    ready_weights()
    near(0, 0)
    rest(0, 0)
    near(0, 1)
    rest(0, 1)
    attend(0, 0)
    attend(0, 1)
    spread(1)
    base_rows()
    gather_group(1, 0)
    gather_group(1, 1)
    base_take(0)
    base_take(1)
    tables(1)
    gather_far(1, 0)
    token_map()
    gather_far(1, 1)
    ready_wo()
    out_weights(1)
    near_out(0, 0)
    base_kept(0)
    rest_out(0, 0)
    base_kept(1)
    near_out(0, 1)
    base_moved(0)
    rest_out(0, 1)
    out_weights(3)
    out_weights(0)
    base_moved(1)
    gather_group(2, 0)
    gather_group(2, 1)
    gather_far(2, 0)
    unlisted(0, 4)
    gather_far(2, 1)
    near(1, 0)
    rest(1, 0)
    near(1, 1)
    rest(1, 1)
    out_weights(2)
    attend(1, 0)
    attend(1, 1)
    unlisted(4, 8)
    ready_ring()
    mix_out(1, 0)
    mix_out(1, 1)
    finish(1, 0)
    write(0)
    finish(1, 1)
    write(1)
    for cp in sends:
        cp.wait_send()


def body(stream, incoming, chosen, live, norm_gain, router, wq, wk, wv, wo):
    half = HD // 2
    freq = np.exp(-math.log(500000.0) * 2.0 * np.arange(half) / HD)
    freq = jnp.asarray(np.concatenate([freq, freq])[None, :], F32)
    vmem = pl.BlockSpec(memory_space=pltpu.VMEM)
    hbm = pl.BlockSpec(memory_space=pl.ANY)
    dma = pltpu.SemaphoreType.DMA
    scratch = [
        pltpu.VMEM((TOKENS, 128), BF16),
        pltpu.VMEM((TOKENS, 128), BF16),
        pltpu.VMEM((TOKENS, 128), BF16),
        pltpu.VMEM((D, 384), BF16),
        pltpu.VMEM((D, 256), BF16),
        pltpu.VMEM((4, 4, 256, 256), BF16),
        pltpu.VMEM((32, D), BF16),
        pltpu.VMEM((32, D), BF16),
        pltpu.VMEM((D, 128), BF16),
        pltpu.VMEM((D, 128), BF16),
        pltpu.VMEM((1, D), F32),
        pltpu.VMEM((1, D), F32),
        pltpu.VMEM((N * H, CAP), BF16),
        pltpu.VMEM((2, CAP), jnp.int32),
        pltpu.VMEM((2, CAP, 128), F32),
        pltpu.VMEM((2, CAP, 128), F32),
        pltpu.VMEM((2, CAP, 128), F32),
        pltpu.VMEM((3, N, 16, H, 256), BF16),
        pltpu.VMEM((N, 4, H, 256), BF16),
        pltpu.VMEM((N, 3, H, 256), BF16),
        pltpu.VMEM((N, 3, H, 256), BF16),
        pltpu.VMEM((2, N, H, 128), BF16),
        pltpu.VMEM((N, H, 256), BF16),
        pltpu.VMEM((2, 2, CAP, 128), BF16),
        pltpu.VMEM((CAP, 128), BF16),
        pltpu.VMEM((CAP, 128), BF16),
        pltpu.VMEM((N, 2 * H, 128), BF16),
        pltpu.VMEM((N, H, 384), F32),
        pltpu.VMEM((N, H, 128), F32),
        pltpu.VMEM((N, H, 128), F32),
        pltpu.VMEM((N, H, 128), F32),
        pltpu.VMEM((N, H, 256), F32),
        pltpu.VMEM((N, H, 256), BF16),
        pltpu.VMEM((N * H, 256), F32),
        pltpu.VMEM((CAP, 256), BF16),
        pltpu.VMEM((N, H, 128), BF16),
        pltpu.VMEM((CAP, 128), BF16),
        pltpu.VMEM((TOKENS, CAP), BF16),
        pltpu.VMEM((TOKENS, 128), F32),
        dma((7,)),
        dma((3, N, 7)),
        dma((3, N, 7)),
        dma((N, 3)),
        dma((N, 3)),
        dma((N, 3)),
        dma((N, 3)),
        dma((4, 2)),
        dma((4, 2)),
        dma((2, N)),
        dma((2, N)),
        dma((2, N, 3)),
        dma((2, N, 3)),
        dma((N, 2)),
        dma((N, 2)),
        dma((5,)),
        dma((5,)),
        dma((N,)),
        dma((N,)),
    ]
    result = pl.pallas_call(
        kernel,
        out_shape=jax.ShapeDtypeStruct((TOKENS, 128), BF16),
        in_specs=[hbm, hbm, vmem, vmem, vmem, vmem, vmem, hbm, hbm, hbm, hbm],
        out_specs=vmem,
        scratch_shapes=scratch,
        compiler_params=pltpu.CompilerParams(
            collective_id=0, has_side_effects=True, vmem_limit_bytes=62 * 2**20
        ),
        name="relay",
    )(stream[0], incoming[0], chosen[0], live, norm_gain, router, freq, wq[0], jnp.swapaxes(wk[0], 0, 1), jnp.swapaxes(wv[0], 0, 1), wo[0])
    return result[None]


def solution(mesh):
    in_specs = (
        P("pipe", None, "tp"),
        P(None, None, "tp"),
        P("pipe", None, None),
        P("pipe", None),
        P("pipe", None),
        P("pipe", None),
        P("pipe", None, "tp"),
        P("pipe", None, "tp"),
        P("pipe", None, "tp"),
        P("pipe", None, "tp"),
    )
    out_specs = P("pipe", None, "tp")
    return jax.shard_map(body, mesh=mesh, in_specs=in_specs, out_specs=out_specs, check_vma=False)
```

time: 110 us -> 105 us (0.955)
  local copies, waits for them, and re-layouts: 6.78 us -> 1.87 us
    unnamed x23 -> x1, local copies, waits for them, and re-layouts: 6.78 us -> 1.87 us
where the time goes in v2:
time: 105 us; the launch traced here: 104 us
  Pallas kernels  103 us (98%)
  local copies, waits for them, and re-layouts  1.87 us (2%)
    pallas_call x1, Pallas kernels, body(): pl.pallas_call(kernel, out_shape=jax.ShapeDtypeStruct((TOKENS, 128), BF16...  103 us

profile of v2, /device:TPU:1, one launch (start us, length us, event | category | flops | bytes accessed | tf_op | source)
XLA Modules:
  0.0 104.4 jit_solution(2038983587793968919)
XLA Ops:
  0.0 102.5 %relay.1 = bf16[2048,128]{1,0:T(8,128)(2,1)} custom-call(bf16[2048,128]{1,0:T(8,128)(2,1)} %bitcast.15, bf16[2048,128]{1,0:T(8,128)(2,1)} %bitcast.16, s32[2,512]{1,0:T(2,128)} %bitcast.19, s32[1,2]{1,0:T(1,128)} %live.1, f32[1,4096]{1,0:T(1,128)} %gain.1, bf16[1,4096]{1,0:T(2,128)(2,1)} %router.1, f32[1,128]{1,0:T(1,128)} %constant.2.clone.freq, ...), custom_call_target="tpu_custom_call" | custom-call | tf_op jit(solution)/shard_map/relay/pallas_call | solution.py:635
  102.5 1.9 %copy.13 = bf16[1,2048,128]{2,1,0:T(8,128)(2,1)} copy(bf16[1,2048,128]{2,1,0:T(8,128)(2,1)} %bitcast.12) | data formatting | bytes 1048576

commit v3 on v2

--- a/solution.py
+++ b/solution.py
@@ -180,19 +180,34 @@
         low, high = value[:H], value[H:]
         return (low * (1 - cf) + high * cf).astype(BF16), (high * (1 - cf) + low * cf).astype(BF16)
 
+    def pass_on(a, g, block):
+        for k, d in ((3, 1), (4, 3)):
+            pltpu.make_async_remote_copy(
+                src_ref=gath.at[a, g, block], dst_ref=gath.at[a, g, block], send_sem=ag_s.at[a, g, k],
+                recv_sem=ag_r.at[a, g, k], device_id=dev(p, (q + d) % 4), device_id_type=MESH,
+            ).start()
+
     def gather_own(a, g):
         for k, d in enumerate((1, 3, 2)):
             put(gath.at[a, g, own], gath.at[a, g, own], ag_s.at[a, g, k], ag_r.at[a, g, k], dev((p + d) % 4, q))
+        pass_on(a, g, own)
 
     def group(qq):
         return pl.ds(qq * 4, 4)
 
     def gather_group(a, g):
         for k, d in enumerate((1, 3, 2)):
-            got(gath.at[a, g, q * 4 + (p + 4 - d) % 4], ag_s.at[a, g, k], ag_r.at[a, g, k])
-        for k, d in ((3, 1), (4, 3)):
+            block = q * 4 + (p + 4 - d) % 4
+            got(gath.at[a, g, block], ag_s.at[a, g, k], ag_r.at[a, g, k])
+            pass_on(a, g, block)
+        for k in (3, 4):
             mine = gath.at[a, g, group(q)]
-            put(mine, mine, ag_s.at[a, g, k], ag_r.at[a, g, k], dev(p, (q + d) % 4))
+            sends.append(
+                pltpu.make_async_remote_copy(
+                    src_ref=mine, dst_ref=mine, send_sem=ag_s.at[a, g, k], recv_sem=ag_r.at[a, g, k],
+                    device_id=partner, device_id_type=MESH,
+                )
+            )
 
     def gather_far(a, g):
         before = (q + 3) % 4
@@ -507,48 +522,48 @@
     gather_group(0, 1)
     place_kv()
     put_out(w2o, w2p, slice(None), 1)
+    tables(0)
     gather_far(0, 0)
     lay_out(wo, woa, loc.at[4])
     put_out(wo, woa, mycols, 2)
-    tables(0)
-    gather_far(0, 1)
     ready_weights()
     near(0, 0)
+    gather_far(0, 1)
+    near(0, 1)
     rest(0, 0)
-    near(0, 1)
     rest(0, 1)
     attend(0, 0)
     attend(0, 1)
     spread(1)
+    gather_group(1, 0)
     base_rows()
-    gather_group(1, 0)
     gather_group(1, 1)
     base_take(0)
     base_take(1)
     tables(1)
     gather_far(1, 0)
+    ready_wo()
+    near_out(0, 0)
+    gather_far(1, 1)
+    near_out(0, 1)
     token_map()
-    gather_far(1, 1)
-    ready_wo()
     out_weights(1)
-    near_out(0, 0)
     base_kept(0)
     rest_out(0, 0)
     base_kept(1)
-    near_out(0, 1)
-    base_moved(0)
     rest_out(0, 1)
     out_weights(3)
     out_weights(0)
+    base_moved(0)
     base_moved(1)
     gather_group(2, 0)
     gather_group(2, 1)
+    unlisted(0, 4)
     gather_far(2, 0)
-    unlisted(0, 4)
+    near(1, 0)
     gather_far(2, 1)
-    near(1, 0)
+    near(1, 1)
     rest(1, 0)
-    near(1, 1)
     rest(1, 1)
     out_weights(2)
     attend(1, 0)
@@ -558,8 +573,8 @@
     mix_out(1, 0)
     mix_out(1, 1)
     finish(1, 0)
+    finish(1, 1)
     write(0)
-    finish(1, 1)
     write(1)
     for cp in sends:
         cp.wait_send()

time: 105 us -> 98.8 us (0.941)
  Pallas kernels: 103 us -> 96.7 us
    pallas_call x1, Pallas kernels: 103 us -> 96.7 us  [body(): pl.pallas_call(kernel, out_shape=jax.ShapeDtypeStruct((TOKENS, 128), BF16...]
where the time goes in v3:
time: 98.8 us; the launch traced here: 98.6 us
  Pallas kernels  96.7 us (98%)
  local copies, waits for them, and re-layouts  1.87 us (2%)
    pallas_call x1, Pallas kernels, body(): pl.pallas_call(kernel, out_shape=jax.ShapeDtypeStruct((TOKENS, 128), BF16...  96.7 us

profile of v3, /device:TPU:1, one launch (start us, length us, event | category | flops | bytes accessed | tf_op | source)
XLA Modules:
  0.0 98.6 jit_solution(17757975388888874358)
XLA Ops:
  0.0 96.7 %relay.1 = bf16[2048,128]{1,0:T(8,128)(2,1)} custom-call(bf16[2048,128]{1,0:T(8,128)(2,1)} %bitcast.15, bf16[2048,128]{1,0:T(8,128)(2,1)} %bitcast.16, s32[2,512]{1,0:T(2,128)} %bitcast.19, s32[1,2]{1,0:T(1,128)} %live.1, f32[1,4096]{1,0:T(1,128)} %gain.1, bf16[1,4096]{1,0:T(2,128)(2,1)} %router.1, f32[1,128]{1,0:T(1,128)} %constant.2.clone.freq, ...), custom_call_target="tpu_custom_call" | custom-call | tf_op jit(solution)/shard_map/relay/pallas_call | solution.py:650
  96.7 1.9 %copy.13 = bf16[1,2048,128]{2,1,0:T(8,128)(2,1)} copy(bf16[1,2048,128]{2,1,0:T(8,128)(2,1)} %bitcast.12) | data formatting | bytes 1048576

commit v4 on v3

--- a/solution.py
+++ b/solution.py
@@ -188,7 +188,7 @@
             ).start()
 
     def gather_own(a, g):
-        for k, d in enumerate((1, 3, 2)):
+        for k, d in ((2, 2), (0, 1), (1, 3)):
             put(gath.at[a, g, own], gath.at[a, g, own], ag_s.at[a, g, k], ag_r.at[a, g, k], dev((p + d) % 4, q))
         pass_on(a, g, own)
 
@@ -307,7 +307,7 @@
             att[g, p, :, 0:128] = result[:H]
             att[g, p, :, 128:256] = result[H:]
             mine = att.at[g, p]
-            for k, d in enumerate((1, 3, 2)):
+            for k, d in ((2, 2), (0, 1), (1, 3)):
                 put(mine, mine, at_s.at[g, k], at_r.at[g, k], dev((p + d) % 4, q))
 
     def out_part(g, shifts, first):

time: 98.8 us -> 97.5 us (0.987)
  Pallas kernels: 96.7 us -> 95.4 us
    pallas_call x1, Pallas kernels: 96.7 us -> 95.4 us  [body(): pl.pallas_call(kernel, out_shape=jax.ShapeDtypeStruct((TOKENS, 128), BF16...]
where the time goes in v4:
time: 97.5 us; the launch traced here: 97.2 us
  Pallas kernels  95.4 us (98%)
  local copies, waits for them, and re-layouts  1.87 us (2%)
    pallas_call x1, Pallas kernels, body(): pl.pallas_call(kernel, out_shape=jax.ShapeDtypeStruct((TOKENS, 128), BF16...  95.4 us

profile of v4, /device:TPU:1, one launch (start us, length us, event | category | flops | bytes accessed | tf_op | source)
XLA Modules:
  0.0 97.2 jit_solution(5931729604524183344)
XLA Ops:
  0.0 95.4 %relay.1 = bf16[2048,128]{1,0:T(8,128)(2,1)} custom-call(bf16[2048,128]{1,0:T(8,128)(2,1)} %bitcast.15, bf16[2048,128]{1,0:T(8,128)(2,1)} %bitcast.16, s32[2,512]{1,0:T(2,128)} %bitcast.19, s32[1,2]{1,0:T(1,128)} %live.1, f32[1,4096]{1,0:T(1,128)} %gain.1, bf16[1,4096]{1,0:T(2,128)(2,1)} %router.1, f32[1,128]{1,0:T(1,128)} %constant.2.clone.freq, ...), custom_call_target="tpu_custom_call" | custom-call | tf_op jit(solution)/shard_map/relay/pallas_call | solution.py:650
  95.4 1.9 %copy.13 = bf16[1,2048,128]{2,1,0:T(8,128)(2,1)} copy(bf16[1,2048,128]{2,1,0:T(8,128)(2,1)} %bitcast.12) | data formatting | bytes 1048576
